TPU v7x, 32 devices: a whole 2x2x4 slice. The times are simulated.
32 devices in a mesh: groups: 2 (over x), expert: 16 (over z, y, core).
Axes of the slice: x: 2, y: 2, z: 4, core: 2. Of those that a mesh axis runs over, the one named last changes fastest.
Arguments:
- tokens: bfloat16 [4096, 896], P(('groups', 'expert')), parts along dimension 0, may hold values from -6 to 6
- routes: int32 [4096, 2], P(('groups', 'expert')), parts along dimension 0, may hold values from 0 to 3, all different within a row; in each aligned block of 128 rows (0 to 127, 128 to 255, ...) at most 80 rows name the same one
- gate_weights: float32 [4096, 2], P(('groups', 'expert')), parts along dimension 0, may hold values from 0.2 to 1
- image_counts: int32 [32, 4], P(('groups', 'expert')), parts along dimension 0, may hold values from 1 to 64, 128 in all within a row
- cotangent: bfloat16 [4096, 896], P(('groups', 'expert')), parts along dimension 0, may hold values from -6 to 6
- up_weight: bfloat16 [16, 896, 1024], P('expert'), may hold values from -0.1875 to 0.1875
- down_weight: bfloat16 [16, 1024, 896], P('expert'), may hold values from -0.09375 to 0.09375
Outputs:
- layer_out: bfloat16 [4096, 896], P(('groups', 'expert')), parts along dimension 0
- token_grad: bfloat16 [4096, 896], P(('groups', 'expert')), parts along dimension 0
- up_grad: bfloat16 [32, 896, 1024], P(('groups', 'expert')), parts along dimension 0
- down_grad: bfloat16 [32, 1024, 896], P(('groups', 'expert')), parts along dimension 0
There are 2 independent parts, one for each index of `groups`. A program takes and returns all parts, laid end to end along the dimension named above; an argument that names none is the same for every part. Nothing has to cross between parts.
Inputs may be any that keep to these rules, and one draw needn't show every extreme that they name: `routes`: in each device's 128 rows no expert is named by more than 80 rows, and in every draw some expert is named by exactly 80 of one device's rows; a row's two experts differ. `image_counts`: each row sums to 128 and its largest entry is 64.
All inputs are finite; a program needn't handle non-finite values.
Results may differ from a plain program's by a relative error of at most 0.0065.
Values may be sent and summed in bfloat16 or wider, within the bound.
A program may use at most 128 MiB of HBM per device.

v0:
```python
import jax
import jax.numpy as jnp
from jax import lax
from jax.sharding import PartitionSpec as P

SPLIT = 4


def gelu_exact(value):
    return 0.5 * value * (1.0 + lax.erf(value * 0.7071067811865476))


def gelu_slope(value):
    return (
        0.5 * (1.0 + lax.erf(value * 0.7071067811865476))
        + value * jnp.exp(-0.5 * value * value) * 0.3989422804014327
    )


def slot_index(routes, capacity, experts):
    flat_routes = routes.reshape(-1)
    onehot = (flat_routes[:, None] == jnp.arange(experts, dtype=jnp.int32)[None, :]).astype(
        jnp.int32
    )
    before = jnp.cumsum(onehot, axis=0) - onehot
    rank = jnp.sum(before * onehot, axis=1)
    return flat_routes * capacity + rank


def fill_slots(slots, values, total):
    pair_ids = jnp.arange(slots.shape[0], dtype=jnp.int32)
    match = slots[None, :] == jnp.arange(total, dtype=jnp.int32)[:, None]
    source = jnp.sum(jnp.where(match, pair_ids[None, :], 0), axis=1)
    filled = jnp.any(match, axis=1)
    return jnp.where(filled[:, None], values[source], jnp.zeros((), values.dtype))


def token_scale(image_counts, tok_count):
    ends = jnp.cumsum(image_counts)
    position = jnp.arange(tok_count, dtype=jnp.int32)
    image = jnp.sum((position[:, None] >= ends[None, :]).astype(jnp.int32), axis=1)
    labels = jnp.arange(image_counts.shape[0], dtype=jnp.int32)
    own = jnp.sum(jnp.where(image[:, None] == labels[None, :], image_counts[None, :], 0), axis=1)
    return tok_count / image_counts.shape[0] / own.astype(jnp.float32)


def prepare_rows(tokens, routes, gate_weights, image_counts, cotangent, experts, capacity):
    tok_count = tokens.shape[0]
    width = tokens.shape[1]
    slots = slot_index(routes, capacity, experts)
    scale = token_scale(image_counts, tok_count)
    x_pairs = jnp.repeat(tokens, 2, axis=0)
    weighted = gate_weights * scale[:, None]
    dy_pairs = (
        (weighted[:, :, None] * cotangent.astype(jnp.float32)[:, None, :])
        .reshape(2 * tok_count, width)
        .astype(jnp.bfloat16)
    )
    total = experts * capacity
    stacked = jnp.stack([fill_slots(slots, x_pairs, total), fill_slots(slots, dy_pairs, total)])
    return (slots, stacked.reshape(2, experts, capacity, width))


def expert_quarter(rows_x, rows_dy, up_part, down_part):
    pre_act = jnp.dot(rows_x, up_part, preferred_element_type=jnp.float32)
    hidden = gelu_exact(pre_act).astype(jnp.bfloat16)
    out_part = jnp.dot(hidden, down_part, preferred_element_type=jnp.float32).astype(jnp.bfloat16)
    back_hidden = jnp.dot(rows_dy, down_part.T, preferred_element_type=jnp.float32)
    back_pre = (back_hidden * gelu_slope(pre_act)).astype(jnp.bfloat16)
    down_part_grad = jnp.dot(hidden.T, rows_dy, preferred_element_type=jnp.float32).astype(
        jnp.bfloat16
    )
    up_part_grad = jnp.dot(rows_x.T, back_pre, preferred_element_type=jnp.float32).astype(
        jnp.bfloat16
    )
    in_part = jnp.dot(back_pre, up_part.T, preferred_element_type=jnp.float32).astype(jnp.bfloat16)
    return (out_part, in_part, up_part_grad, down_part_grad)


def finish_rows(slots, sums, gate_weights):
    flat = sums.reshape(2, -1, sums.shape[-1])
    picked = flat[:, slots]
    tok_count = gate_weights.shape[0]
    outputs = picked[0].reshape(tok_count, 2, -1)
    layer_out = jnp.sum(gate_weights[:, :, None] * outputs, axis=1).astype(jnp.bfloat16)
    token_grad = jnp.sum(picked[1].reshape(tok_count, 2, -1), axis=1).astype(jnp.bfloat16)
    return (layer_out, token_grad)


def local(tokens, routes, gate_weights, image_counts, cotangent, up_weight, down_weight):
    shards = lax.axis_size("expert")
    experts = shards // SPLIT
    tok_count = tokens.shape[0]
    width = tokens.shape[1]
    capacity = SPLIT * ((10 * tok_count + 4 * SPLIT * experts - 1) // (4 * SPLIT * experts))
    slots, stacked = prepare_rows(
        tokens, routes, gate_weights, image_counts[0], cotangent, experts, capacity
    )
    copies = jnp.repeat(stacked, SPLIT, axis=1)
    arrived = lax.all_to_all(copies, "expert", split_axis=1, concat_axis=1, tiled=True)
    rows_x = arrived[0].reshape(-1, width)
    rows_dy = arrived[1].reshape(-1, width)
    out_part, in_part, up_part_grad, down_part_grad = expert_quarter(
        rows_x, rows_dy, up_weight[0], down_weight[0]
    )
    partial_value = jnp.stack([out_part, in_part]).reshape(2, shards, capacity, width)
    returned = lax.all_to_all(partial_value, "expert", split_axis=1, concat_axis=1, tiled=True)
    sums = jnp.sum(returned.reshape(2, experts, SPLIT, capacity, width).astype(jnp.float32), axis=2)
    layer_out, token_grad = finish_rows(slots, sums, gate_weights)
    return (layer_out, token_grad, up_part_grad[None], down_part_grad[None])


def solution(mesh):
    placed = (
        P(("groups", "expert"), None),
        P(("groups", "expert"), None),
        P(("groups", "expert"), None),
        P(("groups", "expert"), None),
        P(("groups", "expert"), None),
        P("expert", None, None),
        P("expert", None, None),
    )
    return jax.shard_map(
        local,
        mesh=mesh,
        in_specs=placed,
        out_specs=(
            P(("groups", "expert"), None),
            P(("groups", "expert"), None),
            P(("groups", "expert"), None, None),
            P(("groups", "expert"), None, None),
        ),
        check_vma=False,
    )
```

profile of v0, /device:TPU:15, one launch (start us, length us, event | category | flops | bytes accessed | tf_op | source)
XLA Modules:
  0.0 279.3 jit_solution(13289824397022332664)
XLA Ops:
  0.6 0.9 copy.34
  1.9 1.2 reduce-window.18
  3.8 0.8 reduce-window.20
  4.7 0.7 select_reduce_fusion.1
  5.5 0.7 broadcast_multiply_fusion.1
  6.5 1.2 broadcast_in_dim.82
  7.7 0.2 reshape.177
  7.9 2.1 mul.107
  10.0 1.8 mul.108
  11.8 2.6 gather_fusion
  14.6 2.2 gather_fusion.1
  16.8 0.2 broadcast_select_fusion.1
  17.2 0.4 broadcast_in_dim.89
  17.6 107.0 %all_to_all.10 = bf16[2,16,80,896]{3,2,0,1:T(8,128)(2,1)S(1)} all-to-all(bf16[2,16,80,896]{3,2,0,1:T(8,128)(2,1)S(1)} %bitcast.64), channel_id=1, replica_groups=mesh['groups'=2,'expert'=16] {'expert'}, dimensions={1} | all-to-all | bytes 9175040 | tf_op jit(solution)/shard_map/all_to_all | solution.py:100
  124.6 0.4 fusion.16
  125.0 5.1 %multiply_convert_fusion = (bf16[1280,1024]{1,0:T(8,128)(2,1)S(1)}, f32[1280,1024]{1,0:T(8,128)S(1)}) fusion(bf16[1280,896]{1,0:T(8,128)(2,1)S(1)} %bitcast.69, bf16[1,896,1024]{2,1,0:T(8,128)(2,1)S(1)} %copy-done), kind=kOutput, calls=%fused_computation.11 | convolution fusion | flops 2355363840 | bytes 11993088 | tf_op jit(solution)/shard_map/dot_general | solution.py:65
  130.1 4.4 %fusion.5 = bf16[1280,1024]{1,0:T(8,128)(2,1)S(1)} fusion(f32[1280,1024]{1,0:T(8,128)S(1)} %get-tuple-element.11, bf16[1280,896]{1,0:T(8,128)(2,1)S(1)} %bitcast.71, bf16[1,1024,896]{2,1,0:T(8,128)(2,1)S(1)} %copy-done.7), kind=kOutput, calls=%fused_computation.10 | convolution fusion | flops 2361917440 | bytes 11993088 | tf_op jit(solution)/shard_map/dot_general | solution.py:68
  134.5 3.1 %convolution_convert_fusion = bf16[1280,896]{1,0:T(8,128)(2,1)S(1)} fusion(bf16[1280,1024]{1,0:T(8,128)(2,1)S(1)} %fusion.5, bf16[1,896,1024]{2,1,0:T(8,128)(2,1)S(1)} %copy-done), kind=kOutput, calls=%fused_computation.14 | convolution fusion | flops 2349957120 | bytes 6750208 | tf_op jit(solution)/shard_map/dot_general | solution.py:76
  137.7 3.1 %convolution_convert_fusion.1 = bf16[1280,896]{1,0:T(8,128)(2,1)S(1)} fusion(bf16[1280,1024]{1,0:T(8,128)(2,1)S(1)} %get-tuple-element.10, bf16[1,1024,896]{2,1,0:T(8,128)(2,1)S(1)} %copy-done.7), kind=kOutput, calls=%fused_computation.15 | convolution fusion | flops 2349957120 | bytes 6750208 | tf_op jit(solution)/shard_map/dot_general | solution.py:67
  140.8 2.6 pad_maximum_fusion
  143.4 5.5 %all-to-all-start.1 = ((bf16[2,16,80,896]{3,2,0,1:T(8,128)(2,1)}), bf16[2,16,80,896]{3,2,0,1:T(8,128)(2,1)}, u32[]{:S(2)}, u32[]{:S(2)}) async-start(bf16[2,16,80,896]{3,2,0,1:T(8,128)(2,1)} %pad_maximum_fusion), calls=%async_computation.1 | async-start | bytes 9175040 | tf_op jit(solution)/shard_map/all_to_all | solution.py:107
  149.3 6.7 %convert_bitcast_fusion = bf16[1,1024,896]{2,1,0:T(8,128)(2,1)} fusion(bf16[1280,1024]{1,0:T(8,128)(2,1)} %copy-done.8, bf16[1280,896]{1,0:T(8,128)(2,1)} %bitcast.72), kind=kOutput, calls=%fused_computation.21 | convolution fusion | flops 2349727744 | bytes 6750208 | tf_op jit(solution)/shard_map/dot_general | solution.py:70
  156.1 3.9 %convert_bitcast_fusion.1 = bf16[1,896,1024]{2,1,0:T(8,128)(2,1)} fusion(bf16[1280,896]{1,0:T(8,128)(2,1)S(1)} %bitcast.70, bf16[1280,1024]{1,0:T(8,128)(2,1)S(1)} %copy-done.10), kind=kOutput, calls=%fused_computation.22 | convolution fusion | flops 2349727744 | bytes 6750208 | tf_op jit(solution)/shard_map/dot_general | solution.py:73
  159.9 89.8 %all-to-all-done.1 = bf16[2,16,80,896]{3,2,0,1:T(8,128)(2,1)} async-done(((bf16[2,16,80,896]{3,2,0,1:T(8,128)(2,1)}), bf16[2,16,80,896]{3,2,0,1:T(8,128)(2,1)}, u32[]{:S(2)}, u32[]{:S(2)}) %all-to-all-start.1) | async-done | bytes 4587552 | tf_op jit(solution)/shard_map/all_to_all | solution.py:107
  249.8 3.2 %convert_reduce_fusion = f32[2,4,80,896]{3,2,0,1:T(8,128)S(1)} fusion(bf16[2,16,80,896]{3,2,0,1:T(8,128)(2,1)} %all-to-all-done.1), kind=kLoop, calls=%fused_computation.3 | loop fusion | flops 4014080 | bytes 6881280 | tf_op jit(solution)/shard_map/reduce_sum | solution.py:108
  253.0 2.6 copy.43
  255.6 5.4 %gather_fusion.2 = f32[256,2,896]{2,1,0:T(2,128)} fusion(f32[2,320,896]{2,0,1:T(2,128)} %bitcast.65, s32[1024]{0:T(1024)S(1)} %pad_clamp_fusion), kind=kCustom, calls=%fused_computation.2 | custom fusion | bytes 3671040 | tf_op jit(solution)/shard_map/gather | solution.py:82
  260.9 8.2 %slice_reduce_fusion = (f32[256,896]{1,0:T(8,128)}, f32[256,896]{1,0:T(8,128)S(1)}) fusion(f32[2,256,896]{2,0,1:T(2,128)} %bitcast.66), kind=kLoop, calls=%fused_computation.24 | loop fusion | bytes 3670016 | tf_op jit(solution)/shard_map/slice | solution.py:86
  269.2 2.7 reshape_squeeze.15
  271.8 1.5 reshape_squeeze.14
  273.3 3.0 %reduce_sum.79 = bf16[128,896]{1,0:T(8,128)(2,1)} reduce(f32[128,2,896]{2,1,0:T(2,128)} %reshape_squeeze.15, f32[]{:T(128)} %constant.12.clone.1), dimensions={1}, to_apply=%region_10.11 | reduce | flops 114688 | bytes 1146884 | tf_op jit(solution)/shard_map/reduce_sum | solution.py:86
  276.3 3.1 %multiply_reduce_fusion = bf16[128,896]{1,0:T(8,128)(2,1)} fusion(f32[128,2,896]{2,1,0:T(2,128)} %reshape_squeeze.14, f32[128,2]{1,0:T(8,128)S(1)} %copy.33), kind=kLoop, calls=%fused_computation.26 | loop fusion | flops 344064 | bytes 1147904 | tf_op jit(solution)/shard_map/reduce_sum | solution.py:85
  (51 shorter events, 2.2 us)
Async XLA Ops:
  0.6 124.4 %copy-start = (bf16[1,896,1024]{2,1,0:T(8,128)(2,1)S(1)}, bf16[1,896,1024]{2,1,0:T(8,128)(2,1)}, u32[]{:S(2)}) copy-start(bf16[1,896,1024]{2,1,0:T(8,128)(2,1)} %param.12) | copy-start | bytes 5505028
  14.6 2.2 copy-start.1
  125.0 5.1 %copy-start.2 = (bf16[1,16,80,896]{3,2,0,1:T(8,128)(2,1)}, bf16[1,16,80,896]{3,2,0,1:T(8,128)(2,1)S(1)}, u32[]{:S(2)}) copy-start(bf16[1,16,80,896]{3,2,0,1:T(8,128)(2,1)S(1)} %get-tuple-element.7) | copy-start | bytes 6881284
  125.0 5.1 %copy-start.4 = (bf16[1,16,80,896]{3,2,0,1:T(8,128)(2,1)}, bf16[1,16,80,896]{3,2,0,1:T(8,128)(2,1)S(1)}, u32[]{:S(2)}) copy-start(bf16[1,16,80,896]{3,2,0,1:T(8,128)(2,1)S(1)} %get-tuple-element.6) | copy-start | bytes 6881284
  125.0 5.1 %copy-start.7 = (bf16[1,1024,896]{2,1,0:T(8,128)(2,1)S(1)}, bf16[1,1024,896]{2,1,0:T(8,128)(2,1)}, u32[]{:S(2)}) copy-start(bf16[1,1024,896]{2,1,0:T(8,128)(2,1)} %param.13) | copy-start | bytes 5505028
  130.1 7.6 %copy-start.8 = (bf16[1280,1024]{1,0:T(8,128)(2,1)}, bf16[1280,1024]{1,0:T(8,128)(2,1)S(1)}, u32[]{:S(2)}) copy-start(bf16[1280,1024]{1,0:T(8,128)(2,1)S(1)} %get-tuple-element.10) | copy-start | bytes 7864324
  134.5 3.2 %copy-start.9 = (bf16[1280,1024]{1,0:T(8,128)(2,1)}, bf16[1280,1024]{1,0:T(8,128)(2,1)S(1)}, u32[]{:S(2)}) copy-start(bf16[1280,1024]{1,0:T(8,128)(2,1)S(1)} %fusion.5) | copy-start | bytes 7864324
  143.4 5.5 %copy-start.5 = (f32[128,2]{0,1:T(2,128)S(1)}, f32[128,2]{0,1:T(2,128)}, u32[]{:S(2)}) copy-start(f32[128,2]{0,1:T(2,128)} %param.9) | copy-start | bytes 3076
  143.4 5.6 %copy-start.6 = (s32[128,2]{0,1:T(2,128)S(1)}, s32[128,2]{0,1:T(2,128)}, u32[]{:S(2)}) copy-start(s32[128,2]{0,1:T(2,128)} %param.8) | copy-start | bytes 3076
  143.4 106.4 %all-to-all-start.1 = ((bf16[2,16,80,896]{3,2,0,1:T(8,128)(2,1)}), bf16[2,16,80,896]{3,2,0,1:T(8,128)(2,1)}, u32[]{:S(2)}, u32[]{:S(2)}) async-start(bf16[2,16,80,896]{3,2,0,1:T(8,128)(2,1)} %pad_maximum_fusion), calls=%async_computation.1 | async-start | bytes 9175040 | tf_op jit(solution)/shard_map/all_to_all | solution.py:107
  149.3 6.8 %copy-start.3 = (bf16[1,16,80,896]{3,2,0,1:T(8,128)(2,1)S(1)}, bf16[1,16,80,896]{3,2,0,1:T(8,128)(2,1)}, u32[]{:S(2)}) copy-start(bf16[1,16,80,896]{3,2,0,1:T(8,128)(2,1)} %copy-done.2) | copy-start | bytes 6881284
  149.3 6.8 %copy-start.10 = (bf16[1280,1024]{1,0:T(8,128)(2,1)S(1)}, bf16[1280,1024]{1,0:T(8,128)(2,1)}, u32[]{:S(2)}) copy-start(bf16[1280,1024]{1,0:T(8,128)(2,1)} %copy-done.9) | copy-start | bytes 7864324
where the time goes:
time: 280 us; the launch traced here: 279 us
  blocking collectives  107 us (38%)
  waiting for transfers between devices  89.8 us (32%)
  local copies, waits for them, and re-layouts  33.4 us (12%)
  matrix products  26.3 us (9%)
  other arithmetic  16.4 us (6%)
  starting transfers between devices  5.49 us (2%)
    all_to_all x1, blocking collectives, local(): lax.all_to_all(copies, 'expert', split_axis=1, concat_axis=1, tiled=True)  107 us
    all_to_all x1, waiting for transfers between devices, local(): lax.all_to_all(partial_value, 'expert', split_axis=1, concat_axis=1, tile...  89.8 us
    slice x1, local copies, waits for them, and re-layouts, finish_rows(): picked[1].reshape(tok_count, 2, -1)  8.21 us
    dot_general x1, matrix products, expert_quarter(): jnp.dot(hidden.T, rows_dy, preferred_element_type=jnp.float32)  6.75 us
  transfers between devices with their start and end apart: 1, of which 1 were waited for; matrix products, arithmetic and copies ran while one was open for 4% of the time, Pallas kernels for 0%

commit v1 on v0

v1 whole, which is shorter than its diff:
```python
import functools

import jax
import jax.numpy as jnp
from jax import lax
from jax.experimental import pallas as pl
from jax.experimental.pallas import tpu as pltpu
from jax.sharding import PartitionSpec as P

SPLIT = 4
TILE = 256
Z, Y, C, F, R1, R2, R3 = range(7)


def kernel(
    experts, rt_ref, gt_ref, cnt_ref, tok_ref, cot_ref, u_hbm, v_hbm,
    lo_ref, tg_ref, ug_hbm, dg_hbm,
    u_ref, v_ref, send, rows, part, t1, t2, ret, hid, back, ug, dg,
    send_sem, recv_sem, w_sem, g_sem,
):
    me = lax.axis_index("expert")
    mine = me // SPLIT
    quarter = lax.rem(me, SPLIT)
    far = mine * SPLIT + lax.rem(quarter + 2, SPLIT)
    near = me + 1 - 2 * lax.rem(me, 2)
    tok, width = tok_ref.shape
    cap = send.shape[2]
    hidden = u_ref.shape[1]
    pieces = hidden // TILE
    bf, f32 = jnp.bfloat16, jnp.float32

    def dest(r):
        return lax.rem(mine - r + experts, experts)

    def source(r):
        return lax.rem(mine + r, experts)

    def copy(src, dst, kind, r, dev):
        return pltpu.make_async_remote_copy(
            src_ref=src, dst_ref=dst,
            send_sem=send_sem.at[kind, r], recv_sem=recv_sem.at[kind, r],
            device_id={"expert": dev}, device_id_type=pl.DeviceIdType.MESH,
        )

    def z_copy(r):
        return copy(send.at[r], rows.at[r, 0], Z, r, dest(r) * SPLIT + quarter)

    def y_copy(r):
        return copy(rows.at[r, 0], rows.at[r, 1], Y, r, far)

    def c_copy(r):
        return copy(rows.at[r, 0], rows.at[r, 2], C, r, near)

    def f_copy(r):
        return copy(rows.at[r, 1], rows.at[r, 3], F, r, near)

    def r1_copy(r):
        return copy(part.at[r, pl.ds(2, 2)], t1.at[r], R1, r, near)

    def r2_copy(r):
        return copy(part.at[r, 1], t2.at[r], R2, r, far)

    def r3_copy(r):
        return copy(part.at[r, 0], ret.at[r], R3, r, source(r) * SPLIT + quarter)

    u_copy = pltpu.make_async_copy(u_hbm.at[0], u_ref, w_sem.at[0])
    v_copy = pltpu.make_async_copy(v_hbm.at[0], v_ref, w_sem.at[1])
    u_copy.start()
    v_copy.start()

    barrier = pltpu.get_barrier_semaphore()
    for r in range(1, experts):
        pl.semaphore_signal(
            barrier, inc=1, device_id={"expert": dest(r) * SPLIT + quarter},
            device_id_type=pl.DeviceIdType.MESH,
        )
    for other in (far, near):
        pl.semaphore_signal(
            barrier, inc=1, device_id={"expert": other}, device_id_type=pl.DeviceIdType.MESH
        )

    heads = max(8, experts)
    row_id = lax.broadcasted_iota(jnp.int32, (heads, tok), 0)
    expert_id = lax.rem(mine - row_id + heads * experts, experts)
    r0 = jnp.broadcast_to(rt_ref[0:1, :], (heads, tok))
    r1 = jnp.broadcast_to(rt_ref[1:2, :], (heads, tok))
    g0 = jnp.broadcast_to(gt_ref[0:1, :], (heads, tok))
    g1 = jnp.broadcast_to(gt_ref[1:2, :], (heads, tok))
    takes0, takes1 = r0 == expert_id, r1 == expert_id
    member = jnp.where(takes0, 1.0, jnp.where(takes1, 1.0, 0.0))
    gate = jnp.where(takes0, g0, jnp.where(takes1, g1, 0.0))
    earlier = jnp.where(
        lax.broadcasted_iota(jnp.int32, (tok, tok), 0)
        < lax.broadcasted_iota(jnp.int32, (tok, tok), 1), 1.0, 0.0)
    rank = jnp.dot(member.astype(bf), earlier.astype(bf), preferred_element_type=f32)
    rank = jnp.where(member > 0.5, rank, -1.0)
    images = cnt_ref.shape[1]
    position = lax.broadcasted_iota(jnp.int32, (heads, tok), 1)
    own = jnp.ones((heads, tok), jnp.int32)
    start = jnp.int32(0)
    for j in range(images):
        count = cnt_ref[0, j]
        own = jnp.where(position >= start, count, own)
        start = start + count
    weight = gate * ((tok / images) / own.astype(f32))
    gate_col = jnp.transpose(gate)
    slot_id = lax.broadcasted_iota(jnp.int32, (cap, tok), 0).astype(f32)

    def choose(r):
        return slot_id == jnp.broadcast_to(rank[r:r + 1], (cap, tok))

    def fill(r, dst):
        hit = choose(r)
        pick = jnp.where(hit, 1.0, 0.0).astype(bf)
        w = jnp.sum(
            jnp.where(hit, jnp.broadcast_to(weight[r:r + 1], (cap, tok)), 0.0),
            axis=1, keepdims=True)
        dst[0] = jnp.dot(pick, tok_ref[...], preferred_element_type=f32).astype(bf)
        dst[1] = (jnp.dot(pick, cot_ref[...], preferred_element_type=f32) * w).astype(bf)

    fill(0, rows.at[0, 0])
    pl.semaphore_wait(barrier, experts + 1)
    y_copy(0).start()
    c_copy(0).start()
    for r in range(1, experts):
        fill(r, send.at[r])
        z_copy(r).start()
    u_copy.wait()
    v_copy.wait()

    def pair_sum(r):
        r1_copy(r).wait_recv()
        for j in (1, 0):
            part[r, j] = (part[r, j].astype(f32) + t1[r, j].astype(f32)).astype(bf)
            if j == 1:
                r2_copy(r).start()

    def step(r, carry):
        @pl.when(r + 1 < experts)
        def _():
            z_copy(r + 1).wait_recv()
            y_copy(r + 1).start()
            c_copy(r + 1).start()

        y_copy(r).wait_recv()
        f_copy(r).start()
        c_copy(r).wait_recv()
        f_copy(r).wait_recv()

        def tile(n, carry):
            col = pl.ds(pl.multiple_of(n * TILE, TILE), TILE)
            x = rows[r, :, 0].reshape(SPLIT * cap, width)
            g = rows[r, :, 1].reshape(SPLIT * cap, width)
            pre = jnp.dot(x, u_ref[:, col], preferred_element_type=f32)
            gv = lax.dot_general(
                g, v_ref[col, :], (((1,), (1,)), ((), ())), preferred_element_type=f32)
            phi = 0.5 * (1.0 + lax.erf(pre * 0.7071067811865476))
            hid[r, :, col] = (pre * phi).astype(bf)
            slope = phi + pre * jnp.exp(-0.5 * pre * pre) * 0.3989422804014327
            back[r, :, col] = (gv * slope).astype(bf)
            return carry

        lax.fori_loop(0, pieces, tile, 0)
        out = jnp.dot(hid[r], v_ref[...], preferred_element_type=f32)
        part[r, :, 0] = out.astype(bf).reshape(SPLIT, cap, width)
        inn = lax.dot_general(
            back[r], u_ref[...], (((1,), (1,)), ((), ())), preferred_element_type=f32)
        part[r, :, 1] = inn.astype(bf).reshape(SPLIT, cap, width)
        r1_copy(r).start()

        @pl.when(r >= 1)
        def _():
            pair_sum(r - 1)

        return carry

    lax.fori_loop(0, experts, step, 0)
    pair_sum(experts - 1)

    def quad_sum(r):
        r2_copy(r).wait_recv()
        part[r, 0] = (part[r, 0].astype(f32) + t2[r].astype(f32)).astype(bf)

        @pl.when(r >= 1)
        def _():
            r3_copy(r).start()

    def ug_copy(n):
        col = pl.ds(pl.multiple_of(n * TILE, TILE), TILE)
        return pltpu.make_async_copy(ug.at[:, col], ug_hbm.at[0, :, col], g_sem.at[0, n])

    def dg_copy(n):
        col = pl.ds(pl.multiple_of(n * TILE, TILE), TILE)
        return pltpu.make_async_copy(dg.at[col, :], dg_hbm.at[0, col, :], g_sem.at[1, n])

    total = experts * SPLIT * cap
    per = -(-experts // pieces)

    def grads(n, carry):
        for j in range(per):
            r = n * per + j

            @pl.when(r < experts)
            def _():
                quad_sum(r)

        col = pl.ds(pl.multiple_of(n * TILE, TILE), TILE)
        x = rows[:, :, 0].reshape(total, width)
        b = back[:, :, col].reshape(total, TILE)
        ug[:, col] = lax.dot_general(
            x, b, (((0,), (0,)), ((), ())), preferred_element_type=f32).astype(bf)
        ug_copy(n).start()
        g = rows[:, :, 1].reshape(total, width)
        h = hid[:, :, col].reshape(total, TILE)
        dg[col, :] = lax.dot_general(
            h, g, (((0,), (0,)), ((), ())), preferred_element_type=f32).astype(bf)
        dg_copy(n).start()
        return carry

    lax.fori_loop(0, pieces, grads, 0)

    layer = jnp.zeros((tok, width), f32)
    grad = jnp.zeros((tok, width), f32)
    for r in range(experts):
        if r:
            r3_copy(r).wait_recv()
        block = ret.at[r] if r else part.at[0, 0]
        pick = jnp.where(choose(r), 1.0, 0.0).astype(bf)
        picked = lax.dot_general(
            pick, block[0], (((0,), (0,)), ((), ())), preferred_element_type=f32)
        layer = layer + picked * gate_col[:, r:r + 1]
        grad = grad + lax.dot_general(
            pick, block[1], (((0,), (0,)), ((), ())), preferred_element_type=f32)
    lo_ref[...] = layer.astype(bf)
    tg_ref[...] = grad.astype(bf)

    def drain(r, carry):
        y_copy(r).wait_send()
        c_copy(r).wait_send()
        f_copy(r).wait_send()
        r1_copy(r).wait_send()
        r2_copy(r).wait_send()

        @pl.when(r >= 1)
        def _():
            z_copy(r).wait_send()
            r3_copy(r).wait_send()

        return carry

    lax.fori_loop(0, experts, drain, 0)

    def drain_grads(n, carry):
        ug_copy(n).wait()
        dg_copy(n).wait()
        return carry

    lax.fori_loop(0, pieces, drain_grads, 0)


def local(tokens, routes, gate_weights, image_counts, cotangent, up_weight, down_weight):
    shards = lax.axis_size("expert")
    experts = shards // SPLIT
    tok, width = tokens.shape
    hidden = up_weight.shape[2]
    capacity = SPLIT * ((10 * tok + 4 * SPLIT * experts - 1) // (4 * SPLIT * experts))
    cap = -(-capacity // 16) * 16
    bf = jnp.bfloat16
    vmem = pl.BlockSpec(memory_space=pltpu.VMEM)
    smem = pl.BlockSpec(memory_space=pltpu.SMEM)
    hbm = pl.BlockSpec(memory_space=pl.ANY)
    rows = experts * SPLIT * cap
    return pl.pallas_call(
        functools.partial(kernel, experts),
        out_shape=(
            jax.ShapeDtypeStruct((tok, width), bf),
            jax.ShapeDtypeStruct((tok, width), bf),
            jax.ShapeDtypeStruct((1, width, hidden), bf),
            jax.ShapeDtypeStruct((1, hidden, width), bf),
        ),
        in_specs=[vmem, vmem, smem, vmem, vmem, hbm, hbm],
        out_specs=(vmem, vmem, hbm, hbm),
        scratch_shapes=[
            pltpu.VMEM((width, hidden), bf),
            pltpu.VMEM((hidden, width), bf),
            pltpu.VMEM((experts, 2, cap, width), bf),
            pltpu.VMEM((experts, SPLIT, 2, cap, width), bf),
            pltpu.VMEM((experts, SPLIT, 2, cap, width), bf),
            pltpu.VMEM((experts, 2, 2, cap, width), bf),
            pltpu.VMEM((experts, 2, cap, width), bf),
            pltpu.VMEM((experts, 2, cap, width), bf),
            pltpu.VMEM((experts, SPLIT * cap, hidden), bf),
            pltpu.VMEM((experts, SPLIT * cap, hidden), bf),
            pltpu.VMEM((width, hidden), bf),
            pltpu.VMEM((hidden, width), bf),
            pltpu.SemaphoreType.DMA((7, experts)),
            pltpu.SemaphoreType.DMA((7, experts)),
            pltpu.SemaphoreType.DMA((2,)),
            pltpu.SemaphoreType.DMA((2, hidden // TILE)),
        ],
        compiler_params=pltpu.CompilerParams(
            collective_id=0, has_side_effects=True, vmem_limit_bytes=58 * 1024 * 1024
        ),
        cost_estimate=pl.CostEstimate(
            flops=12 * rows * width * hidden,
            bytes_accessed=8 * width * hidden,
            transcendentals=2 * rows * hidden,
        ),
    )(routes.T, gate_weights.T, image_counts, tokens, cotangent, up_weight, down_weight)


def solution(mesh):
    placed = (
        P(("groups", "expert"), None),
        P(("groups", "expert"), None),
        P(("groups", "expert"), None),
        P(("groups", "expert"), None),
        P(("groups", "expert"), None),
        P("expert", None, None),
        P("expert", None, None),
    )
    return jax.shard_map(
        local,
        mesh=mesh,
        in_specs=placed,
        out_specs=(
            P(("groups", "expert"), None),
            P(("groups", "expert"), None),
            P(("groups", "expert"), None, None),
            P(("groups", "expert"), None, None),
        ),
        check_vma=False,
    )
```

time: 280 us -> 95.7 us (0.34)
  the two profiles are of different devices: /device:TPU:15 before, /device:TPU:26 now
where the time goes in v1:
time: 95.7 us; the launch traced here: 95.5 us
  Pallas kernels  87.3 us (91%)
  local copies, waits for them, and re-layouts  7.53 us (8%)
    pallas_call x1, Pallas kernels, local(): pl.pallas_call(functools.partial(kernel, experts), out_shape=(jax.ShapeDt...  87.3 us
    unnamed x6, local copies, waits for them, and re-layouts  7.53 us

profile of v1, /device:TPU:26, one launch (start us, length us, event | category | flops | bytes accessed | tf_op | source)
XLA Modules:
  0.0 95.5 jit_solution(4557515950856637902)
XLA Ops:
  0.6 87.3 %shard_map.102 = (bf16[128,896]{1,0:T(8,128)(2,1)}, bf16[128,896]{1,0:T(8,128)(2,1)}, bf16[1,896,1024]{2,1,0:T(8,128)(2,1)}, bf16[1,1024,896]{2,1,0:T(8,128)(2,1)}) custom-call(s32[2,128]{1,0:T(2,128)} %bitcast.2, f32[2,128]{1,0:T(2,128)} %bitcast.3, s32[1,4]{1,0:T(1,128)} %cnt_ref.1, bf16[128,896]{1,0:T(8,128)(2,1)} %tok_ref.1, bf16[128,896]{1,0:T(8,128)(2,1)} %cot_ref.1, ...), custom_call_target="tpu_custom_call" | custom-call | flops 14092861440 | bytes 7340032 | tf_op jit(solution)/shard_map/pallas_call | solution.py:273
  88.0 1.6 %copy.15 = bf16[128,896]{1,0:T(8,128)(2,1)} copy(bf16[128,896]{1,0:T(8,128)(2,1)} %get-tuple-element.8) | data formatting | bytes 458752
  89.6 1.6 %copy.16 = bf16[128,896]{1,0:T(8,128)(2,1)} copy(bf16[128,896]{1,0:T(8,128)(2,1)} %get-tuple-element.9) | data formatting | bytes 458752
  91.2 0.0 copy-start
  91.2 3.0 %copy.17 = bf16[1,896,1024]{2,1,0:T(8,128)(2,1)} copy(bf16[1,896,1024]{2,1,0:T(8,128)(2,1)} %get-tuple-element.10) | data formatting | bytes 3670016
  94.3 0.0 copy-done
  94.3 1.2 %copy.18 = bf16[1,1024,896]{2,1,0:T(8,128)(2,1)} copy(bf16[1,1024,896]{2,1,0:T(8,128)(2,1)S(1)} %copy-done) | data formatting | bytes 3670016
Async XLA Ops:
  91.2 3.0 %copy-start = (bf16[1,1024,896]{2,1,0:T(8,128)(2,1)S(1)}, bf16[1,1024,896]{2,1,0:T(8,128)(2,1)}, u32[]{:S(2)}) copy-start(bf16[1,1024,896]{2,1,0:T(8,128)(2,1)} %get-tuple-element.11) | copy-start | bytes 5505028

commit v2 on v1

--- a/solution.py
+++ b/solution.py
@@ -29,11 +29,21 @@
     pieces = hidden // TILE
     bf, f32 = jnp.bfloat16, jnp.float32
 
+    def turn(r):
+        half = (r + 1) // 2
+        return half if r % 2 else experts - half
+
+    def turn_of(r):
+        if isinstance(r, int):
+            return turn(r)
+        half = (r + 1) // 2
+        return jnp.where(lax.rem(r, 2) == 1, half, experts - half)
+
     def dest(r):
-        return lax.rem(mine - r + experts, experts)
+        return lax.rem(mine - turn_of(r) + experts, experts)
 
     def source(r):
-        return lax.rem(mine + r, experts)
+        return lax.rem(mine + turn_of(r), experts)
 
     def copy(src, dst, kind, r, dev):
         return pltpu.make_async_remote_copy(
@@ -81,7 +91,7 @@
 
     heads = max(8, experts)
     row_id = lax.broadcasted_iota(jnp.int32, (heads, tok), 0)
-    expert_id = lax.rem(mine - row_id + heads * experts, experts)
+    expert_id = lax.rem(mine - turn_of(row_id) + heads * experts, experts)
     r0 = jnp.broadcast_to(rt_ref[0:1, :], (heads, tok))
     r1 = jnp.broadcast_to(rt_ref[1:2, :], (heads, tok))
     g0 = jnp.broadcast_to(gt_ref[0:1, :], (heads, tok))
@@ -124,7 +134,10 @@
     c_copy(0).start()
     for r in range(1, experts):
         fill(r, send.at[r])
-        z_copy(r).start()
+        if r == 1:
+            z_copy(1).start()
+    z_copy(1).wait_send()
+    z_copy(2).start()
     u_copy.wait()
     v_copy.wait()
 
@@ -135,6 +148,14 @@
             if j == 1:
                 r2_copy(r).start()
 
+    def quad_sum(r):
+        r2_copy(r).wait_recv()
+        part[r, 0] = (part[r, 0].astype(f32) + t2[r].astype(f32)).astype(bf)
+
+        @pl.when(jnp.int32(r) >= 1)
+        def _():
+            r3_copy(r).start()
+
     def step(r, carry):
         @pl.when(r + 1 < experts)
         def _():
@@ -144,6 +165,15 @@
 
         y_copy(r).wait_recv()
         f_copy(r).start()
+
+        @pl.when(r >= 1)
+        def _():
+            pair_sum(r - 1)
+
+        @pl.when(r >= 2)
+        def _():
+            quad_sum(r - 2)
+
         c_copy(r).wait_recv()
         f_copy(r).wait_recv()
 
@@ -161,30 +191,21 @@
             return carry
 
         lax.fori_loop(0, pieces, tile, 0)
+
+        @pl.when(r + 3 < experts)
+        def _():
+            z_copy(r + 2).wait_send()
+            z_copy(r + 3).start()
+
         out = jnp.dot(hid[r], v_ref[...], preferred_element_type=f32)
         part[r, :, 0] = out.astype(bf).reshape(SPLIT, cap, width)
         inn = lax.dot_general(
             back[r], u_ref[...], (((1,), (1,)), ((), ())), preferred_element_type=f32)
         part[r, :, 1] = inn.astype(bf).reshape(SPLIT, cap, width)
         r1_copy(r).start()
-
-        @pl.when(r >= 1)
-        def _():
-            pair_sum(r - 1)
-
         return carry
 
     lax.fori_loop(0, experts, step, 0)
-    pair_sum(experts - 1)
-
-    def quad_sum(r):
-        r2_copy(r).wait_recv()
-        part[r, 0] = (part[r, 0].astype(f32) + t2[r].astype(f32)).astype(bf)
-
-        @pl.when(r >= 1)
-        def _():
-            r3_copy(r).start()
-
     def ug_copy(n):
         col = pl.ds(pl.multiple_of(n * TILE, TILE), TILE)
         return pltpu.make_async_copy(ug.at[:, col], ug_hbm.at[0, :, col], g_sem.at[0, n])
@@ -194,15 +215,16 @@
         return pltpu.make_async_copy(dg.at[col, :], dg_hbm.at[0, col, :], g_sem.at[1, n])
 
     total = experts * SPLIT * cap
-    per = -(-experts // pieces)
 
     def grads(n, carry):
-        for j in range(per):
-            r = n * per + j
-
-            @pl.when(r < experts)
-            def _():
-                quad_sum(r)
+        @pl.when(n == 1)
+        def _():
+            pair_sum(experts - 1)
+            quad_sum(experts - 2)
+
+        @pl.when(n == pieces - 1)
+        def _():
+            quad_sum(experts - 1)
 
         col = pl.ds(pl.multiple_of(n * TILE, TILE), TILE)
         x = rows[:, :, 0].reshape(total, width)
@@ -243,12 +265,12 @@
 
         @pl.when(r >= 1)
         def _():
-            z_copy(r).wait_send()
             r3_copy(r).wait_send()
 
         return carry
 
     lax.fori_loop(0, experts, drain, 0)
+    z_copy(experts - 1).wait_send()
 
     def drain_grads(n, carry):
         ug_copy(n).wait()

time: 95.7 us -> 86.8 us (0.907)
  the two profiles are of different devices: /device:TPU:26 before, /device:TPU:0 now
where the time goes in v2:
time: 86.8 us; the launch traced here: 86.6 us
  Pallas kernels  78.5 us (90%)
  local copies, waits for them, and re-layouts  7.53 us (9%)
    pallas_call x1, Pallas kernels, local(): pl.pallas_call(functools.partial(kernel, experts), out_shape=(jax.ShapeDt...  78.5 us
    unnamed x6, local copies, waits for them, and re-layouts  7.53 us

profile of v2, /device:TPU:0, one launch (start us, length us, event | category | flops | bytes accessed | tf_op | source)
XLA Modules:
  0.0 86.6 jit_solution(5989820063685415010)
XLA Ops:
  0.6 78.5 %shard_map.102 = (bf16[128,896]{1,0:T(8,128)(2,1)}, bf16[128,896]{1,0:T(8,128)(2,1)}, bf16[1,896,1024]{2,1,0:T(8,128)(2,1)}, bf16[1,1024,896]{2,1,0:T(8,128)(2,1)}) custom-call(s32[2,128]{1,0:T(2,128)} %bitcast.2, f32[2,128]{1,0:T(2,128)} %bitcast.3, s32[1,4]{1,0:T(1,128)} %cnt_ref.1, bf16[128,896]{1,0:T(8,128)(2,1)} %tok_ref.1, bf16[128,896]{1,0:T(8,128)(2,1)} %cot_ref.1, ...), custom_call_target="tpu_custom_call" | custom-call | flops 14092861440 | bytes 7340032 | tf_op jit(solution)/shard_map/pallas_call | solution.py:295
  79.1 1.6 %copy.15 = bf16[128,896]{1,0:T(8,128)(2,1)} copy(bf16[128,896]{1,0:T(8,128)(2,1)} %get-tuple-element.8) | data formatting | bytes 458752
  80.8 1.6 %copy.16 = bf16[128,896]{1,0:T(8,128)(2,1)} copy(bf16[128,896]{1,0:T(8,128)(2,1)} %get-tuple-element.9) | data formatting | bytes 458752
  82.4 0.0 copy-start
  82.4 3.0 %copy.17 = bf16[1,896,1024]{2,1,0:T(8,128)(2,1)} copy(bf16[1,896,1024]{2,1,0:T(8,128)(2,1)} %get-tuple-element.10) | data formatting | bytes 3670016
  85.4 0.0 copy-done
  85.4 1.2 %copy.18 = bf16[1,1024,896]{2,1,0:T(8,128)(2,1)} copy(bf16[1,1024,896]{2,1,0:T(8,128)(2,1)S(1)} %copy-done) | data formatting | bytes 3670016
Async XLA Ops:
  82.4 3.0 %copy-start = (bf16[1,1024,896]{2,1,0:T(8,128)(2,1)S(1)}, bf16[1,1024,896]{2,1,0:T(8,128)(2,1)}, u32[]{:S(2)}) copy-start(bf16[1,1024,896]{2,1,0:T(8,128)(2,1)} %get-tuple-element.11) | copy-start | bytes 5505028

commit v3 on v2

--- a/solution.py
+++ b/solution.py
@@ -45,33 +45,33 @@
     def source(r):
         return lax.rem(mine + turn_of(r), experts)
 
-    def copy(src, dst, kind, r, dev):
+    def copy(src, dst, kind, r, h, dev):
         return pltpu.make_async_remote_copy(
             src_ref=src, dst_ref=dst,
-            send_sem=send_sem.at[kind, r], recv_sem=recv_sem.at[kind, r],
+            send_sem=send_sem.at[kind, r, h], recv_sem=recv_sem.at[kind, r, h],
             device_id={"expert": dev}, device_id_type=pl.DeviceIdType.MESH,
         )
 
-    def z_copy(r):
-        return copy(send.at[r], rows.at[r, 0], Z, r, dest(r) * SPLIT + quarter)
-
-    def y_copy(r):
-        return copy(rows.at[r, 0], rows.at[r, 1], Y, r, far)
-
-    def c_copy(r):
-        return copy(rows.at[r, 0], rows.at[r, 2], C, r, near)
-
-    def f_copy(r):
-        return copy(rows.at[r, 1], rows.at[r, 3], F, r, near)
-
-    def r1_copy(r):
-        return copy(part.at[r, pl.ds(2, 2)], t1.at[r], R1, r, near)
-
-    def r2_copy(r):
-        return copy(part.at[r, 1], t2.at[r], R2, r, far)
-
-    def r3_copy(r):
-        return copy(part.at[r, 0], ret.at[r], R3, r, source(r) * SPLIT + quarter)
+    def z_copy(r, h):
+        return copy(send.at[r, h], rows.at[r, 0, h], Z, r, h, dest(r) * SPLIT + quarter)
+
+    def y_copy(r, h):
+        return copy(rows.at[r, 0, h], rows.at[r, 1, h], Y, r, h, far)
+
+    def c_copy(r, h):
+        return copy(rows.at[r, 0, h], rows.at[r, 2, h], C, r, h, near)
+
+    def f_copy(r, h):
+        return copy(rows.at[r, 1, h], rows.at[r, 3, h], F, r, h, near)
+
+    def r1_copy(r, h):
+        return copy(part.at[r, pl.ds(2, 2), h], t1.at[r, :, h], R1, r, h, near)
+
+    def r2_copy(r, h):
+        return copy(part.at[r, 1, h], t2.at[r, h], R2, r, h, far)
+
+    def r3_copy(r, h):
+        return copy(part.at[r, 0, h], ret.at[r, h], R3, r, h, source(r) * SPLIT + quarter)
 
     u_copy = pltpu.make_async_copy(u_hbm.at[0], u_ref, w_sem.at[0])
     v_copy = pltpu.make_async_copy(v_hbm.at[0], v_ref, w_sem.at[1])
@@ -119,63 +119,79 @@
     def choose(r):
         return slot_id == jnp.broadcast_to(rank[r:r + 1], (cap, tok))
 
-    def fill(r, dst):
+    def fill(r, dst, send_half):
         hit = choose(r)
         pick = jnp.where(hit, 1.0, 0.0).astype(bf)
+        dst[0] = jnp.dot(pick, tok_ref[...], preferred_element_type=f32).astype(bf)
+        send_half(0)
         w = jnp.sum(
             jnp.where(hit, jnp.broadcast_to(weight[r:r + 1], (cap, tok)), 0.0),
             axis=1, keepdims=True)
-        dst[0] = jnp.dot(pick, tok_ref[...], preferred_element_type=f32).astype(bf)
         dst[1] = (jnp.dot(pick, cot_ref[...], preferred_element_type=f32) * w).astype(bf)
-
-    fill(0, rows.at[0, 0])
+        send_half(1)
+
+    def send_own(h):
+        y_copy(0, h).start()
+        c_copy(0, h).start()
+
+    def send_first(h):
+        z_copy(1, h).start()
+
     pl.semaphore_wait(barrier, experts + 1)
-    y_copy(0).start()
-    c_copy(0).start()
-    for r in range(1, experts):
-        fill(r, send.at[r])
-        if r == 1:
-            z_copy(1).start()
-    z_copy(1).wait_send()
-    z_copy(2).start()
+    fill(1, send.at[1], send_first)
+    fill(0, rows.at[0, 0], send_own)
+    for r in range(2, experts):
+        fill(r, send.at[r], lambda h: None)
+    for h in range(2):
+        z_copy(1, h).wait_send()
+        z_copy(2, h).start()
     u_copy.wait()
     v_copy.wait()
 
     def pair_sum(r):
-        r1_copy(r).wait_recv()
-        for j in (1, 0):
-            part[r, j] = (part[r, j].astype(f32) + t1[r, j].astype(f32)).astype(bf)
-            if j == 1:
-                r2_copy(r).start()
-
-    def quad_sum(r):
-        r2_copy(r).wait_recv()
-        part[r, 0] = (part[r, 0].astype(f32) + t2[r].astype(f32)).astype(bf)
+        for h in range(2):
+            r1_copy(r, h).wait_recv()
+            for j in (1, 0):
+                part[r, j, h] = (part[r, j, h].astype(f32) + t1[r, j, h].astype(f32)).astype(bf)
+                if j == 1:
+                    r2_copy(r, h).start()
+
+    def quad_sum(r, h):
+        r2_copy(r, h).wait_recv()
+        part[r, 0, h] = (part[r, 0, h].astype(f32) + t2[r, h].astype(f32)).astype(bf)
 
         @pl.when(jnp.int32(r) >= 1)
         def _():
-            r3_copy(r).start()
+            r3_copy(r, h).start()
 
     def step(r, carry):
+        for h in range(2):
+            y_copy(r, h).wait_recv()
+            f_copy(r, h).start()
+
+        @pl.when(r >= 2)
+        def _():
+            pair_sum(r - 1)
+
         @pl.when(r + 1 < experts)
         def _():
-            z_copy(r + 1).wait_recv()
-            y_copy(r + 1).start()
-            c_copy(r + 1).start()
-
-        y_copy(r).wait_recv()
-        f_copy(r).start()
-
-        @pl.when(r >= 1)
-        def _():
-            pair_sum(r - 1)
+            for h in range(2):
+                z_copy(r + 1, h).wait_recv()
+                y_copy(r + 1, h).start()
+                c_copy(r + 1, h).start()
+
+        @pl.when(r == 1)
+        def _():
+            pair_sum(0)
 
         @pl.when(r >= 2)
         def _():
-            quad_sum(r - 2)
-
-        c_copy(r).wait_recv()
-        f_copy(r).wait_recv()
+            for h in range(2):
+                quad_sum(r - 2, h)
+
+        for h in range(2):
+            c_copy(r, h).wait_recv()
+            f_copy(r, h).wait_recv()
 
         def tile(n, carry):
             col = pl.ds(pl.multiple_of(n * TILE, TILE), TILE)
@@ -194,15 +210,17 @@
 
         @pl.when(r + 3 < experts)
         def _():
-            z_copy(r + 2).wait_send()
-            z_copy(r + 3).start()
+            for h in range(2):
+                z_copy(r + 2, h).wait_send()
+                z_copy(r + 3, h).start()
 
         out = jnp.dot(hid[r], v_ref[...], preferred_element_type=f32)
         part[r, :, 0] = out.astype(bf).reshape(SPLIT, cap, width)
+        r1_copy(r, 0).start()
         inn = lax.dot_general(
             back[r], u_ref[...], (((1,), (1,)), ((), ())), preferred_element_type=f32)
         part[r, :, 1] = inn.astype(bf).reshape(SPLIT, cap, width)
-        r1_copy(r).start()
+        r1_copy(r, 1).start()
         return carry
 
     lax.fori_loop(0, experts, step, 0)
@@ -220,11 +238,12 @@
         @pl.when(n == 1)
         def _():
             pair_sum(experts - 1)
-            quad_sum(experts - 2)
+            for h in range(2):
+                quad_sum(experts - 2, h)
 
         @pl.when(n == pieces - 1)
         def _():
-            quad_sum(experts - 1)
+            quad_sum(experts - 1, 0)
 
         col = pl.ds(pl.multiple_of(n * TILE, TILE), TILE)
         x = rows[:, :, 0].reshape(total, width)
@@ -240,37 +259,42 @@
         return carry
 
     lax.fori_loop(0, pieces, grads, 0)
+    quad_sum(experts - 1, 1)
 
     layer = jnp.zeros((tok, width), f32)
     grad = jnp.zeros((tok, width), f32)
     for r in range(experts):
         if r:
-            r3_copy(r).wait_recv()
+            r3_copy(r, 0).wait_recv()
         block = ret.at[r] if r else part.at[0, 0]
         pick = jnp.where(choose(r), 1.0, 0.0).astype(bf)
         picked = lax.dot_general(
             pick, block[0], (((0,), (0,)), ((), ())), preferred_element_type=f32)
         layer = layer + picked * gate_col[:, r:r + 1]
+        if r:
+            r3_copy(r, 1).wait_recv()
         grad = grad + lax.dot_general(
             pick, block[1], (((0,), (0,)), ((), ())), preferred_element_type=f32)
     lo_ref[...] = layer.astype(bf)
     tg_ref[...] = grad.astype(bf)
 
     def drain(r, carry):
-        y_copy(r).wait_send()
-        c_copy(r).wait_send()
-        f_copy(r).wait_send()
-        r1_copy(r).wait_send()
-        r2_copy(r).wait_send()
-
-        @pl.when(r >= 1)
-        def _():
-            r3_copy(r).wait_send()
+        for h in range(2):
+            y_copy(r, h).wait_send()
+            c_copy(r, h).wait_send()
+            f_copy(r, h).wait_send()
+            r1_copy(r, h).wait_send()
+            r2_copy(r, h).wait_send()
+
+            @pl.when(r >= 1)
+            def _():
+                r3_copy(r, h).wait_send()
 
         return carry
 
     lax.fori_loop(0, experts, drain, 0)
-    z_copy(experts - 1).wait_send()
+    for h in range(2):
+        z_copy(experts - 1, h).wait_send()
 
     def drain_grads(n, carry):
         ug_copy(n).wait()
@@ -315,8 +339,8 @@
             pltpu.VMEM((experts, SPLIT * cap, hidden), bf),
             pltpu.VMEM((width, hidden), bf),
             pltpu.VMEM((hidden, width), bf),
-            pltpu.SemaphoreType.DMA((7, experts)),
-            pltpu.SemaphoreType.DMA((7, experts)),
+            pltpu.SemaphoreType.DMA((7, experts, 2)),
+            pltpu.SemaphoreType.DMA((7, experts, 2)),
             pltpu.SemaphoreType.DMA((2,)),
             pltpu.SemaphoreType.DMA((2, hidden // TILE)),
         ],

time: 86.8 us -> 86.6 us (level)
  no operation moved by 1% of the time
where the time goes in v3:
time: 86.6 us; the launch traced here: 86.4 us
  Pallas kernels  78.2 us (90%)
  local copies, waits for them, and re-layouts  7.53 us (9%)
    pallas_call x1, Pallas kernels, local(): pl.pallas_call(functools.partial(kernel, experts), out_shape=(jax.ShapeDt...  78.2 us
    unnamed x6, local copies, waits for them, and re-layouts  7.53 us

profile of v3, /device:TPU:0, one launch (start us, length us, event | category | flops | bytes accessed | tf_op | source)
XLA Modules:
  0.0 86.4 jit_solution(8558759717271598558)
XLA Ops:
  0.6 78.2 %shard_map.102 = (bf16[128,896]{1,0:T(8,128)(2,1)}, bf16[128,896]{1,0:T(8,128)(2,1)}, bf16[1,896,1024]{2,1,0:T(8,128)(2,1)}, bf16[1,1024,896]{2,1,0:T(8,128)(2,1)}) custom-call(s32[2,128]{1,0:T(2,128)} %bitcast.2, f32[2,128]{1,0:T(2,128)} %bitcast.3, s32[1,4]{1,0:T(1,128)} %cnt_ref.1, bf16[128,896]{1,0:T(8,128)(2,1)} %tok_ref.1, bf16[128,896]{1,0:T(8,128)(2,1)} %cot_ref.1, ...), custom_call_target="tpu_custom_call" | custom-call | flops 14092861440 | bytes 7340032 | tf_op jit(solution)/shard_map/pallas_call | solution.py:319
  78.9 1.6 %copy.15 = bf16[128,896]{1,0:T(8,128)(2,1)} copy(bf16[128,896]{1,0:T(8,128)(2,1)} %get-tuple-element.8) | data formatting | bytes 458752
  80.5 1.6 %copy.16 = bf16[128,896]{1,0:T(8,128)(2,1)} copy(bf16[128,896]{1,0:T(8,128)(2,1)} %get-tuple-element.9) | data formatting | bytes 458752
  82.1 0.0 copy-start
  82.1 3.0 %copy.17 = bf16[1,896,1024]{2,1,0:T(8,128)(2,1)} copy(bf16[1,896,1024]{2,1,0:T(8,128)(2,1)} %get-tuple-element.10) | data formatting | bytes 3670016
  85.2 0.0 copy-done
  85.2 1.2 %copy.18 = bf16[1,1024,896]{2,1,0:T(8,128)(2,1)} copy(bf16[1,1024,896]{2,1,0:T(8,128)(2,1)S(1)} %copy-done) | data formatting | bytes 3670016
Async XLA Ops:
  82.1 3.0 %copy-start = (bf16[1,1024,896]{2,1,0:T(8,128)(2,1)S(1)}, bf16[1,1024,896]{2,1,0:T(8,128)(2,1)}, u32[]{:S(2)}) copy-start(bf16[1,1024,896]{2,1,0:T(8,128)(2,1)} %get-tuple-element.11) | copy-start | bytes 5505028

commit v4 on v3

--- a/solution.py
+++ b/solution.py
@@ -135,9 +135,10 @@
         c_copy(0, h).start()
 
     def send_first(h):
+        if h == 0:
+            pl.semaphore_wait(barrier, experts + 1)
         z_copy(1, h).start()
 
-    pl.semaphore_wait(barrier, experts + 1)
     fill(1, send.at[1], send_first)
     fill(0, rows.at[0, 0], send_own)
     for r in range(2, experts):

time: 86.6 us -> 86.4 us (level)
  no operation moved by 1% of the time
where the time goes in v4:
time: 86.4 us; the launch traced here: 86.2 us
  Pallas kernels  78 us (90%)
  local copies, waits for them, and re-layouts  7.53 us (9%)
    pallas_call x1, Pallas kernels, local(): pl.pallas_call(functools.partial(kernel, experts), out_shape=(jax.ShapeDt...  78 us
    unnamed x6, local copies, waits for them, and re-layouts  7.53 us

profile of v4, /device:TPU:0, one launch (start us, length us, event | category | flops | bytes accessed | tf_op | source)
XLA Modules:
  0.0 86.2 jit_solution(9684262501603649712)
XLA Ops:
  0.6 78.0 %shard_map.102 = (bf16[128,896]{1,0:T(8,128)(2,1)}, bf16[128,896]{1,0:T(8,128)(2,1)}, bf16[1,896,1024]{2,1,0:T(8,128)(2,1)}, bf16[1,1024,896]{2,1,0:T(8,128)(2,1)}) custom-call(s32[2,128]{1,0:T(2,128)} %bitcast.2, f32[2,128]{1,0:T(2,128)} %bitcast.3, s32[1,4]{1,0:T(1,128)} %cnt_ref.1, bf16[128,896]{1,0:T(8,128)(2,1)} %tok_ref.1, bf16[128,896]{1,0:T(8,128)(2,1)} %cot_ref.1, ...), custom_call_target="tpu_custom_call" | custom-call | flops 14092861440 | bytes 7340032 | tf_op jit(solution)/shard_map/pallas_call | solution.py:320
  78.7 1.6 %copy.15 = bf16[128,896]{1,0:T(8,128)(2,1)} copy(bf16[128,896]{1,0:T(8,128)(2,1)} %get-tuple-element.8) | data formatting | bytes 458752
  80.3 1.6 %copy.16 = bf16[128,896]{1,0:T(8,128)(2,1)} copy(bf16[128,896]{1,0:T(8,128)(2,1)} %get-tuple-element.9) | data formatting | bytes 458752
  82.0 0.0 copy-start
  82.0 3.0 %copy.17 = bf16[1,896,1024]{2,1,0:T(8,128)(2,1)} copy(bf16[1,896,1024]{2,1,0:T(8,128)(2,1)} %get-tuple-element.10) | data formatting | bytes 3670016
  85.0 0.0 copy-done
  85.0 1.2 %copy.18 = bf16[1,1024,896]{2,1,0:T(8,128)(2,1)} copy(bf16[1,1024,896]{2,1,0:T(8,128)(2,1)S(1)} %copy-done) | data formatting | bytes 3670016
Async XLA Ops:
  82.0 3.0 %copy-start = (bf16[1,1024,896]{2,1,0:T(8,128)(2,1)S(1)}, bf16[1,1024,896]{2,1,0:T(8,128)(2,1)}, u32[]{:S(2)}) copy-start(bf16[1,1024,896]{2,1,0:T(8,128)(2,1)} %get-tuple-element.11) | copy-start | bytes 5505028
